TPU v7x, 256 devices: a whole 4x4x8 slice. The times are simulated.
256 devices in a mesh: bl: 32 (over x, y, core), lst: 8 (over z).
Axes of the slice: x: 4, y: 4, z: 8, core: 2. Of those that a mesh axis runs over, the one named last changes fastest.
Arguments:
- visibility: bfloat16 [1024, 128, 2, 1536], P('bl', 'lst'), may hold values from -6 to 6
- channel_flags: int32 [128, 1536], P('lst'), may hold values 0 or 1
- time_bins: int32 [128], P('lst'), may hold values from 0 to 15
- baseline_group_index: int32 [1024], replicated, may hold values from 0 to 63, as said below
- owner_map: int32 [64], replicated, may hold values from 0 to 63, as said below
Outputs:
- delay_power: float32 [64, 16, 1536], P('bl', 'lst')
Inputs may be any that keep to these rules, and one draw needn't show every extreme that they name: `baseline_group_index`: every group holds 2 or more baselines. Of the 32 baselines of one index of bl, at most 2 lie in groups of one owner, the owner of group g being owner_map[g] // 2; some index of bl has exactly 2 for some owner, and some owner receives exactly 2 from every index of bl. `owner_map`: A permutation of the groups.
All inputs are finite; a program needn't handle non-finite values. No bound on the sum of `channel_flags` on one device may be relied on, other than what follows from the above.
Results may differ from a plain program's by a relative error of at most 0.0068.
Values may be sent and summed in bfloat16 or wider, within the bound.
A program may use at most 128 MiB of HBM per device.

v0:
```python
import math

import jax
import jax.numpy as jnp
from jax import lax
from jax.sharding import PartitionSpec as P

BINS_DEV = 2


def taper_weights(channel_flags, channels):
    channel_axis = jnp.arange(channels, dtype=jnp.int32).astype(jnp.float32)
    phase = channel_axis * (2.0 * math.pi / channels)
    taper = (
        0.35875
        - 0.48829 * jnp.cos(phase)
        + 0.14128 * jnp.cos(2.0 * phase)
        - 0.01168 * jnp.cos(3.0 * phase)
    )
    return taper[None, :] * channel_flags.astype(jnp.float32)


def dft_tables(channels):
    counter = jnp.arange(channels, dtype=jnp.int32)
    product = counter[:, None] * counter[None, :] % channels
    angle = product.astype(jnp.float32) * (2.0 * math.pi / channels)
    factor = 1.0 / math.sqrt(channels)
    return (
        (jnp.cos(angle) * factor).astype(jnp.bfloat16),
        (jnp.sin(angle) * factor).astype(jnp.bfloat16),
    )


def transform(samples, weights, cos_table, sin_table):
    baseline_total_count, time_count, _, channels = samples.shape
    tapered = (samples.astype(jnp.float32) * weights[None, :, None, :]).astype(jnp.bfloat16)
    flat = tapered.reshape(-1, channels)
    along_cos = jnp.dot(flat, cos_table, preferred_element_type=jnp.float32).reshape(
        baseline_total_count, time_count, 2, channels
    )
    along_sin = jnp.dot(flat, sin_table, preferred_element_type=jnp.float32).reshape(
        baseline_total_count, time_count, 2, channels
    )
    real_part = along_cos[:, :, 0] + along_sin[:, :, 1]
    imag_part = along_cos[:, :, 1] - along_sin[:, :, 0]
    return jnp.stack([real_part, imag_part], axis=2).astype(jnp.bfloat16)


def group_power(members, member_table, inverse_pairs):
    member_count, time_count, _, delays = members.shape
    group_count = member_table.shape[0]
    summed = jnp.dot(
        member_table.astype(jnp.bfloat16),
        members.reshape(member_count, -1),
        preferred_element_type=jnp.float32,
    )
    summed = summed.reshape(group_count, time_count, 2, delays)
    real_part = members[:, :, 0].astype(jnp.float32)
    imag_part = members[:, :, 1].astype(jnp.float32)
    magnitude = (real_part * real_part + imag_part * imag_part).reshape(member_count, -1)
    squares = jnp.dot(member_table, magnitude, precision=lax.Precision.HIGHEST).reshape(
        group_count, time_count, delays
    )
    total = summed[:, :, 0] * summed[:, :, 0] + summed[:, :, 1] * summed[:, :, 1]
    return (total - squares) * inverse_pairs[:, None, None]


def binned_sample_times(cross, bin_table):
    return jnp.einsum("qtk,tj->qjk", cross, bin_table, precision=lax.Precision.HIGHEST)


def accumulate(binned):
    total = lax.psum(binned, "lst")
    return lax.dynamic_slice_in_dim(total, lax.axis_index("lst") * BINS_DEV, BINS_DEV, 1)


def on_device(visibility, channel_flags, time_bins, baseline_group_index, owner_map):
    baseline_total_count, time_count, _, channels = visibility.shape
    bl_count = lax.axis_size("bl")
    lst_count = lax.axis_size("lst")
    group_capacity = max(2, 2 * baseline_total_count // bl_count)
    group_count = owner_map.shape[0]
    own_groups = group_count // bl_count
    bin_count = BINS_DEV * lst_count
    every_baseline_list = baseline_group_index.shape[0]
    cos_table, sin_table = dft_tables(channels)
    spectra = transform(visibility, taper_weights(channel_flags, channels), cos_table, sin_table)
    rows = owner_map[baseline_group_index]
    row_table = (rows[:, None] == jnp.arange(group_count, dtype=jnp.int32)[None, :]).astype(
        jnp.float32
    )
    counts = jnp.sum(row_table, axis=0)
    inverse_pairs = 1.0 / (counts * (counts - 1.0))
    bin_table = (time_bins[:, None] == jnp.arange(bin_count, dtype=jnp.int32)[None, :]).astype(
        jnp.float32
    )
    device_index = lax.axis_index("bl")
    owners = rows // own_groups
    owner_onehot = (owners[:, None] == jnp.arange(bl_count, dtype=jnp.int32)[None, :]).astype(
        jnp.int32
    )
    owner_onehot = owner_onehot.reshape(bl_count, baseline_total_count, bl_count)
    before = jnp.cumsum(owner_onehot, axis=1) - owner_onehot
    member_ranks = jnp.sum(before * owner_onehot, axis=2).reshape(-1)
    send_slot = lax.dynamic_slice_in_dim(
        owners * group_capacity + member_ranks,
        device_index * baseline_total_count,
        baseline_total_count,
        0,
    )
    dispatch = (
        jnp.arange(bl_count * group_capacity, dtype=jnp.int32)[:, None] == send_slot[None, :]
    ).astype(jnp.bfloat16)
    outgoing = jnp.dot(
        dispatch, spectra.reshape(baseline_total_count, -1), preferred_element_type=jnp.float32
    )
    outgoing = outgoing.astype(jnp.bfloat16).reshape(
        bl_count, group_capacity, time_count, 2, channels
    )
    sender_position = (
        jnp.arange(every_baseline_list, dtype=jnp.int32) // baseline_total_count * group_capacity
        + member_ranks
    )
    slot_table = (
        sender_position[:, None] == jnp.arange(bl_count * group_capacity, dtype=jnp.int32)[None, :]
    ).astype(jnp.float32)
    mine_table = lax.dynamic_slice_in_dim(row_table, device_index * own_groups, own_groups, 1)
    receive_map = jnp.dot(mine_table.T, slot_table, precision=lax.Precision.HIGHEST)
    mine_pairs = lax.dynamic_slice_in_dim(inverse_pairs, device_index * own_groups, own_groups, 0)
    received = lax.all_to_all(outgoing, "bl", split_axis=0, concat_axis=0, tiled=True)
    pieces = received.shape[2]
    members = received.reshape(bl_count * group_capacity, pieces, 2, channels)
    cross = group_power(members, receive_map, mine_pairs)
    return accumulate(binned_sample_times(cross, bin_table))


def solution(mesh):
    in_specs = (P("bl", "lst", None, None), P("lst", None), P("lst"), P(), P())
    out_specs = P("bl", "lst", None)
    return jax.shard_map(
        on_device, mesh=mesh, in_specs=in_specs, out_specs=out_specs, check_vma=False
    )
```

profile of v0, /device:TPU:2, one launch (start us, length us, event | category | flops | bytes accessed | tf_op | source)
XLA Modules:
  0.0 433.5 jit_solution(6650933024615620643)
XLA Ops:
  6.5 0.0 copy-start.3
  6.5 0.0 copy-start.4
  6.5 0.0 copy-start.1
  6.5 0.1 multiply_subtract_fusion
  6.6 36.9 %fusion.84 = bf16[1536,1536,1,1]{1,0,3,2:T(8,128)(2,1)S(1)} fusion(), kind=kLoop, calls=%fused_computation.18.clone.clone.1 | loop fusion | flops 25952256 | bytes 4718592 | tf_op jit(solution)/shard_map/dot_general | solution.py:41
  43.5 37.1 %fusion.86 = bf16[1536,1536,1,1]{1,0,3,2:T(8,128)(2,1)S(1)} fusion(), kind=kLoop, calls=%fused_computation.17.clone.clone.1 | loop fusion | flops 25952256 | bytes 4718592 | tf_op jit(solution)/shard_map/dot_general | solution.py:38
  80.6 0.0 copy-done.3
  80.6 0.7 fusion.75
  81.3 0.7 fusion.72
  82.0 0.7 fusion.73
  82.7 0.7 fusion.74
  83.5 0.0 copy-done.4
  83.5 0.0 copy-done.1
  83.5 4.9 %multiply_convert_fusion.2 = bf16[32,16,2,1536]{3,2,1,0:T(2,128)(2,1)} fusion(bf16[32,16,2,1536]{3,2,1,0:T(2,128)(2,1)S(1)} %copy-done.1, f32[16,1536]{1,0:T(8,128)S(1)} %convert_multiply_fusion), kind=kLoop, calls=%fused_computation.16 | loop fusion | flops 4718592 | bytes 6389760 | tf_op jit(solution)/shard_map/convert_element_type | solution.py:36
  88.4 0.0 copy-start.2
  88.4 7.1 %fusion.12 = f32[32,16,2,1536]{3,1,2,0:T(8,128)S(1)} fusion(bf16[32,16,2,1536]{3,2,1,0:T(2,128)(2,1)} %multiply_convert_fusion.2, bf16[1536,1536,1,1]{1,0,3,2:T(8,128)(2,1)S(1)} %fusion.84), kind=kOutput, calls=%fused_computation.19 | convolution fusion | flops 4831838208 | bytes 14155776 | tf_op jit(solution)/shard_map/dot_general | solution.py:41
  95.5 0.0 copy-done.2
  95.5 5.0 %fusion.14 = f32[32,16,2,1536]{3,1,2,0:T(8,128)S(1)} fusion(bf16[32,16,2,1536]{3,2,1,0:T(2,128)(2,1)S(1)} %copy-done.2, bf16[1536,1536,1,1]{1,0,3,2:T(8,128)(2,1)S(1)} %fusion.86), kind=kOutput, calls=%fused_computation.20 | convolution fusion | flops 4831838208 | bytes 14155776 | tf_op jit(solution)/shard_map/dot_general | solution.py:38
  100.6 1.8 fusion.25
  102.4 0.3 pad_maximum_fusion
  102.7 0.0 copy-start.5
  102.7 3.4 copy.35
  106.1 3.6 convert_element_type.67
  109.7 0.0 copy-done.5
  109.7 39.6 %select_select_fusion = s32[1024]{0:T(1024)S(1)} fusion(s32[1024]{0:T(1024)S(1)} %copy-done.5, s32[]{:T(128)} %bitcast.1, s32[]{:T(128)} %bitcast.2, s32[]{:T(128)} %bitcast.3, s32[]{:T(128)} %bitcast.4, s32[]{:T(128)} %bitcast.5, s32[]{:T(128)} %bitcast.6, s32[]{:T(128)} %bitcast.7, s32[]{:T(128)} %bitcast.8, s32[]{:T(128)} %bitcast.9, s32[]{:T(128)} %bitcast.10, ...), kind=kLoop, calls=%fused_computation.82 | loop fusion | flops 132096 | bytes 8448 | tf_op jit(solution)/shard_map/gather | solution.py:88
  149.3 0.1 gather.6
  149.4 0.1 copy.31
  149.5 1.0 fusion.76
  150.5 0.1 copy.32
  150.6 0.1 reshape.101
  150.7 39.6 %fusion.49 = (s32[1024]{0:T(1024)S(1)}, s32[1024]{0:T(1024)S(1)}) fusion(s32[1024]{0:T(1024)S(1)} %reshape.101, s32[]{:T(128)} %bitcast.64, s32[]{:T(128)} %bitcast.63, s32[]{:T(128)} %bitcast.62, s32[]{:T(128)} %bitcast.61, s32[]{:T(128)} %bitcast.60, s32[]{:T(128)} %bitcast.59, s32[]{:T(128)} %bitcast.58, s32[]{:T(128)} %bitcast.57, s32[]{:T(128)} %bitcast.56, ...), kind=kLoop, calls=%fused_computation.76 | loop fusion | flops 159744 | bytes 16640 | tf_op jit(solution)/shard_map/add | solution.py:121
  190.3 0.1 dynamic_slice.13
  190.4 6.3 %convolution_convert_fusion = bf16[64,49152]{1,0:T(8,128)(2,1)} fusion(bf16[32,49152]{1,0:T(8,128)(2,1)} %convert_element_type.67, s32[32]{0:T(128)S(1)} %dynamic_slice.13), kind=kOutput, calls=%fused_computation | convolution fusion | flops 204474368 | bytes 9437312 | tf_op jit(solution)/shard_map/dot_general | solution.py:114
  196.7 9.6 %reshape.102 = bf16[32,2,16,2,1536]{4,3,2,1,0:T(2,128)(2,1)} reshape(bf16[64,49152]{1,0:T(8,128)(2,1)} %convolution_convert_fusion) | data formatting | bytes 12582912 | tf_op jit(solution)/shard_map/reshape | solution.py:117
  206.3 7.7 %all-to-all-start = ((bf16[32,2,16,2,1536]{4,3,2,1,0:T(2,128)(2,1)}), bf16[32,2,16,2,1536]{4,3,2,1,0:T(2,128)(2,1)}, u32[]{:S(2)}, u32[]{:S(2)}) async-start(bf16[32,2,16,2,1536]{4,3,2,1,0:T(2,128)(2,1)} %reshape.102), calls=%async_computation | async-start | bytes 12582912 | tf_op jit(solution)/shard_map/all_to_all | solution.py:130
  213.9 0.0 all-reduce.2.cloned.1.call-start
  214.0 0.1 convert_reduce_fusion
  214.1 0.1 dynamic_slice.14
  214.3 0.3 fusion.36
  214.6 76.3 %all-to-all-done = bf16[32,2,16,2,1536]{4,3,2,1,0:T(2,128)(2,1)} async-done(((bf16[32,2,16,2,1536]{4,3,2,1,0:T(2,128)(2,1)}), bf16[32,2,16,2,1536]{4,3,2,1,0:T(2,128)(2,1)}, u32[]{:S(2)}, u32[]{:S(2)}) %all-to-all-start) | async-done | bytes 6291488 | tf_op jit(solution)/shard_map/all_to_all | solution.py:130
  290.9 9.5 %reshape_reshape.3 = bf16[64,49152]{1,0:T(8,128)(2,1)} reshape(bf16[32,2,16,2,1536]{4,3,2,1,0:T(2,128)(2,1)} %all-to-all-done) | data formatting | bytes 12582912 | tf_op jit(solution)/shard_map/reshape;reshape | solution.py:54
  300.3 9.6 %dot_general.34 = bf16[16,2,1536,64]{2,1,0,3:T(2,128)(2,1)} reshape(bf16[49152,64]{0,1:T(8,128)(2,1)} %bitcast.121) | data formatting | bytes 12582912 | tf_op jit(solution)/shard_map/dot_general | solution.py:52
  309.9 0.0 copy-start
  309.9 15.1 %fusion.71 = (bf16[64,16,1,1536]{3,2,1,0:T(2,128)(2,1)S(1)}, bf16[64,16,1,1536]{3,2,1,0:T(2,128)(2,1)S(1)}) fusion(bf16[64,16,2,1536]{3,2,1,0:T(2,128)(2,1)} %bitcast.74), kind=kLoop, calls=%fused_computation.102 | loop fusion | bytes 12582912 | tf_op jit(solution)/shard_map/slice | solution.py:58
  325.1 0.0 copy-done
  325.1 6.7 %fusion.8 = f32[2,16,2,1536]{3,0,2,1:T(2,128)S(1)} fusion(bf16[16,2,1536,64]{2,1,0,3:T(2,128)(2,1)S(1)} %copy-done, f32[2,64]{1,0:T(2,128)S(1)} %fusion.36), kind=kOutput, calls=%fused_computation.13 | convolution fusion | flops 12583040 | bytes 6685184 | tf_op jit(solution)/shard_map/dot_general | solution.py:52
  331.8 2.1 multiply_add_fusion
  333.9 0.0 copy-start.6
  333.9 6.8 %fusion.31 = f32[2,16,1536]{2,0,1:T(2,128)S(1)} fusion(f32[2,16,2,1536]{3,0,2,1:T(2,128)S(1)} %fusion.8, f32[2]{0:T(128)S(1)} %dynamic_slice.14, f32[2,64]{1,0:T(2,128)S(1)} %fusion.36, f32[8,8,16,1536]{3,2,1,0:T(8,128)S(1)} %bitcast.122), kind=kOutput, calls=%fused_computation.35 | convolution fusion | flops 37994496 | bytes 6881800 | tf_op jit(solution)/shard_map/dot_general | solution.py:61
  340.7 0.0 copy-done.6
  340.7 0.9 convolution_bitcast_fusion
  341.6 0.0 all-reduce.2.cloned.1.call-update
  341.6 83.2 %all-reduce.2.cloned.1.call-done = f32[2,16,1536]{2,1,0:T(8,128)} async-done(((f32[2,16,1536]{2,1,0:T(8,128)}), f32[2,16,1536]{2,1,0:T(8,128)}) %all-reduce.2.cloned.1.call-update) | async-done | bytes 196624 | tf_op jit(solution)/shard_map/psum | solution.py:73
  424.9 1.5 constant_dynamic-slice_fusion
  (4 shorter events, 0.1 us)
Async XLA Ops:
  6.5 74.1 %copy-start.3 = (s32[64]{0:T(128)S(1)}, s32[64]{0:T(128)}, u32[]{:S(2)}) copy-start(s32[64]{0:T(128)} %param.9) | copy-start | bytes 772
  6.5 76.9 %copy-start.4 = (s32[16,1536]{1,0:T(8,128)S(1)}, s32[16,1536]{1,0:T(8,128)}, u32[]{:S(2)}) copy-start(s32[16,1536]{1,0:T(8,128)} %param.6) | copy-start | bytes 294916
  6.5 77.0 %copy-start.1 = (bf16[32,16,2,1536]{3,2,1,0:T(2,128)(2,1)S(1)}, bf16[32,16,2,1536]{3,2,1,0:T(2,128)(2,1)}, u32[]{:S(2)}) copy-start(bf16[32,16,2,1536]{3,2,1,0:T(2,128)(2,1)} %param.5) | copy-start | bytes 9437188
  88.4 7.1 %copy-start.2 = (bf16[32,16,2,1536]{3,2,1,0:T(2,128)(2,1)S(1)}, bf16[32,16,2,1536]{3,2,1,0:T(2,128)(2,1)}, u32[]{:S(2)}) copy-start(bf16[32,16,2,1536]{3,2,1,0:T(2,128)(2,1)} %multiply_convert_fusion.2) | copy-start | bytes 9437188
  102.7 7.1 %copy-start.5 = (s32[1024]{0:T(1024)S(1)}, s32[1024]{0:T(1024)}, u32[]{:S(2)}) copy-start(s32[1024]{0:T(1024)} %param.8) | copy-start | bytes 12292
  206.3 84.6 %all-to-all-start = ((bf16[32,2,16,2,1536]{4,3,2,1,0:T(2,128)(2,1)}), bf16[32,2,16,2,1536]{4,3,2,1,0:T(2,128)(2,1)}, u32[]{:S(2)}, u32[]{:S(2)}) async-start(bf16[32,2,16,2,1536]{4,3,2,1,0:T(2,128)(2,1)} %reshape.102), calls=%async_computation | async-start | bytes 12582912 | tf_op jit(solution)/shard_map/all_to_all | solution.py:130
  213.9 210.9 %all-reduce.2.cloned.1.call-start = ((), (), s32[]{:S(2)}) async-start(), calls=%async_computation.1 | async-start | bytes 393216 | tf_op jit(solution)/shard_map/psum | solution.py:73
  309.9 15.2 %copy-start = (bf16[16,2,1536,64]{2,1,0,3:T(2,128)(2,1)S(1)}, bf16[16,2,1536,64]{2,1,0,3:T(2,128)(2,1)}, u32[]{:S(2)}) copy-start(bf16[16,2,1536,64]{2,1,0,3:T(2,128)(2,1)} %dot_general.34) | copy-start | bytes 18874372
  333.9 6.8 %copy-start.6 = (s32[16]{0:T(128)S(1)}, s32[16]{0:T(128)}, u32[]{:S(2)}) copy-start(s32[16]{0:T(128)} %param.7) | copy-start | bytes 196
Sparse Core Ops, SparseCore 0:
  341.7 83.0 all-reduce.1
where the time goes:
time: 439 us; the launch traced here: 433 us
  other arithmetic  164 us (37%)
  waiting for transfers between devices  160 us (36%)
  local copies, waits for them, and re-layouts  55.7 us (13%)
  matrix products  33.1 us (8%)
  between operations  13.9 us (3%)
  starting transfers between devices  7.71 us (2%)
    psum x1, waiting for transfers between devices, accumulate(): total = lax.psum(binned, 'lst')  83.2 us
    all_to_all x1, waiting for transfers between devices, on_device(): lax.all_to_all(outgoing, 'bl', split_axis=0, concat_axis=0, tiled=True)  76.3 us
    add x1, other arithmetic, on_device(): jnp.arange(every_baseline_list, dtype=jnp.int32) // baseline_total_count  39.6 us
    gather x1, other arithmetic, on_device(): rows = owner_map[baseline_group_index]  39.6 us
    dot_general x1, other arithmetic, transform(): jnp.dot(flat, cos_table, preferred_element_type=jnp.float32)  37.1 us
    dot_general x1, other arithmetic, transform(): jnp.dot(flat, sin_table, preferred_element_type=jnp.float32)  36.9 us
    slice x1, local copies, waits for them, and re-layouts, group_power(): real_part = members[:, :, 0].astype(jnp.float32)  15.1 us
    reshape x1, local copies, waits for them, and re-layouts, on_device(): outgoing.astype(jnp.bfloat16)  9.6 us
  transfers between devices with their start and end apart: 2, of which 2 were waited for; matrix products, arithmetic and copies ran while one was open for 0% of the time, Pallas kernels for 0%

commit v1 on v0

v1 whole, which is shorter than its diff:
```python
import functools
import math

import jax
import jax.numpy as jnp
import numpy as np
from jax import lax
from jax.experimental import pallas as pl
from jax.experimental.pallas import tpu as pltpu
from jax.sharding import PartitionSpec as P

MESH = pl.DeviceIdType.MESH
F = 1536
H = F // 2
NC = 3
NB = 32
PIECES = 4
PB = NB // PIECES
BF = jnp.bfloat16
F32 = jnp.float32


def tables():
    f = np.arange(H, dtype=np.int64)[:, None]
    m = np.arange(H // 2, dtype=np.int64)[None, :]
    out = np.zeros((2, H, NC, 2, 128), np.float32)
    for parity in range(2):
        k = 2 * m + parity
        angle = 2.0 * np.pi * ((f * k) % F) / F
        cos, sin = np.cos(angle), np.sin(angle)
        if parity == 0:
            sin[:, 0] = np.cos(np.pi * f[:, 0])
        out[parity, :, :, 0] = (cos / math.sqrt(F)).reshape(H, NC, 128)
        out[parity, :, :, 1] = (sin / math.sqrt(F)).reshape(H, NC, 128)
    return out.reshape(2, H, NC * 256).astype(jnp.bfloat16)


def taper_row():
    phase = np.arange(F, dtype=np.float32) * np.float32(2.0 * math.pi / F)
    phase = phase.astype(np.float64)
    taper = (
        0.35875
        - 0.48829 * np.cos(phase)
        + 0.14128 * np.cos(2.0 * phase)
        - 0.01168 * np.cos(3.0 * phase)
    )
    return taper.astype(np.float32)[None, :]


def kernel(
    idx_ref, inv_ref, vis_ref, tab_hbm, flags_ref, taper_ref, bins_ref,
    out_ref,
    xv, w2, yall, ysend, tab, ra, rb, planes, send1, recv1, send2, recv2, power, zsend, zrecv,
    ld_sem, tab_sem, ys_sem, yr_sem, s1_sem, r1_sem, s2_sem, r2_sem, zs_sem, zr_sem,
):
    bl = lax.axis_index("bl")
    z = lax.axis_index("lst")
    c = lax.rem(bl, 2)
    y = lax.rem(bl // 2, 4)
    x = bl // 8

    def at(xx, yy, cc, zz):
        return (xx * 8 + yy * 2 + cc, zz)

    def x_peer(d):
        return at(lax.rem(x + d, 4), y, c, z)

    def y_peer(d):
        return at(x, lax.rem(y + d, 4), c, z)

    def z_peer(d, e):
        return at(x, y, lax.rem(c + e, 2), lax.rem(z + d, 8))

    z_offsets = [(d, e) for d in range(8) for e in range(2) if d or e]

    rows = vis_ref.reshape(NB, 32, F)
    loads = []
    for p in range(PIECES):
        cp = pltpu.make_async_copy(
            rows.at[pl.ds(p * PB, PB)], xv.at[pl.ds(p * PB, PB)], ld_sem.at[p]
        )
        cp.start()
        loads.append(cp)
    tab_cp = pltpu.make_async_copy(tab_hbm.at[c], tab, tab_sem)
    tab_cp.start()

    barrier = pltpu.get_barrier_semaphore()
    peers = [z_peer(d, e) for d, e in z_offsets]
    peers += [x_peer(d) for d in (1, 2, 3)] + [y_peer(d) for d in (1, 2, 3)]
    for peer in peers:
        pl.semaphore_signal(barrier, inc=1, device_id=peer, device_id_type=MESH)

    for t in range(16):
        row = taper_ref[...] * flags_ref[pl.ds(t, 1), :].astype(F32)
        w2[pl.ds(2 * t, 2), :] = jnp.broadcast_to(row, (2, F))
    planes[2 * NB] = jnp.zeros((6, 16, 128), F32)
    sign = (1 - 2 * c).astype(F32)

    pl.semaphore_wait(barrier, len(peers))
    exchange = []
    for p in range(PIECES):
        loads[p].wait()

        def fold(b, carry):
            for j in range(6):
                lo_at, hi_at = pl.ds(j * 128, 128), pl.ds(H + j * 128, 128)
                lo = (xv[b, :, lo_at].astype(F32) * w2[:, lo_at]).astype(BF).astype(F32)
                hi = (xv[b, :, hi_at].astype(F32) * w2[:, hi_at]).astype(BF).astype(F32)
                hi = hi * sign
                at_rows = pl.ds(pl.multiple_of(b * 32, 32), 32)
                yall[0, at_rows, lo_at] = (lo + hi).astype(BF)
                ysend[at_rows, lo_at] = (lo - hi).astype(BF)
            return carry

        lax.fori_loop(p * PB, (p + 1) * PB, fold, 0)
        piece = pl.ds(p * PB * 32, PB * 32)
        cp = pltpu.make_async_remote_copy(
            src_ref=ysend.at[piece],
            dst_ref=yall.at[1, piece],
            send_sem=ys_sem.at[p],
            recv_sem=yr_sem.at[p],
            device_id=z_peer(0, 1),
            device_id_type=MESH,
        )
        cp.start()
        exchange.append(cp)
    tab_cp.wait()

    def first(half, n, d):
        peer = x_peer(d) if half == 0 else y_peer(d)
        mine = x if half == 0 else y
        return pltpu.make_async_remote_copy(
            src_ref=send1.at[half, n, lax.rem(mine + d, 4)],
            dst_ref=recv1.at[half, n, d - 1],
            send_sem=s1_sem.at[half, n, d - 1],
            recv_sem=r1_sem.at[half, n, d - 1],
            device_id=peer,
            device_id_type=MESH,
        )

    def second(half, n, d):
        peer = y_peer(d) if half == 0 else x_peer(d)
        mine = y if half == 0 else x
        return pltpu.make_async_remote_copy(
            src_ref=send2.at[half, n, lax.rem(mine + d, 4)],
            dst_ref=recv2.at[half, n, d - 1],
            send_sem=s2_sem.at[half, n, d - 1],
            recv_sem=r2_sem.at[half, n, d - 1],
            device_id=peer,
            device_id_type=MESH,
        )

    lane = lax.broadcasted_iota(jnp.int32, (1, 128), 1)
    for n in range(NC):
        special = (lane + c) == 0
        for side in range(2):
            if side == 1 and n == 0:
                for cp in exchange:
                    cp.wait_recv()

            def transform(i, carry):
                at_rows = pl.ds(pl.multiple_of(i * 512, 512), 512)
                prod = jnp.dot(
                    yall[side, at_rows, :],
                    tab[:, pl.ds(n * 256, 256)],
                    preferred_element_type=F32,
                )
                ra[...] = prod[:, :128]
                rb[...] = prod[:, 128:]

                def split(b, carry):
                    start = b * 32
                    ar = ra[pl.ds(start, 16, stride=2), :]
                    ai = ra[pl.ds(start + 1, 16, stride=2), :]
                    br = rb[pl.ds(start, 16, stride=2), :]
                    bi = rb[pl.ds(start + 1, 16, stride=2), :]
                    if n == 0:
                        zero = jnp.zeros_like(ar)
                        pr = ar + jnp.where(special, zero, bi)
                        pi = ai - jnp.where(special, zero, br)
                        mr = jnp.where(special, br, ar - bi)
                        mi = jnp.where(special, bi, ai + br)
                    else:
                        pr, pi, mr, mi = ar + bi, ai - br, ar - bi, ai + br
                    at_b = side * NB + i * 16 + b
                    planes[at_b, 0] = pr
                    planes[at_b, 1] = pi
                    planes[at_b, 2] = pr * pr + pi * pi
                    planes[at_b, 3] = mr
                    planes[at_b, 4] = mi
                    planes[at_b, 5] = mr * mr + mi * mi
                    return carry

                return lax.fori_loop(0, 16, split, carry)

            lax.fori_loop(0, 2, transform, 0)

        def gather(q, carry):
            members = [idx_ref[q, s] for s in range(4)]
            qx, qy, qg = q // 16, lax.rem(q // 4, 4), lax.rem(q, 4)
            for plane in range(6):
                total = planes[members[0], plane] + planes[members[1], plane]
                total += planes[members[2], plane] + planes[members[3], plane]
                total = total.astype(BF)
                if plane < 3:
                    send1[0, n, qx, qy * 4 + qg, plane] = total
                else:
                    send1[1, n, qy, qx * 4 + qg, plane - 3] = total
            return carry

        lax.fori_loop(0, 64, gather, 0)
        for d in (2, 1, 3):
            for half in range(2):
                first(half, n, d).start()

    for n in range(NC):
        for half in range(2):
            for d in (1, 2, 3):
                first(half, n, d).wait_recv()
            mine = x if half == 0 else y

            def combine(i, carry):
                total = send1[half, n, mine, i].astype(F32)
                for d in (1, 2, 3):
                    total += recv1[half, n, d - 1, i].astype(F32)
                send2[half, n, i // 4, lax.rem(i, 4)] = total.astype(BF)
                return carry

            lax.fori_loop(0, 16, combine, 0)
            for d in (2, 1, 3):
                second(half, n, d).start()

    for n in range(NC):
        for half in range(2):
            for d in (1, 2, 3):
                second(half, n, d).wait_recv()
            mine = y if half == 0 else x

            def finish(g, carry):
                total = send2[half, n, mine, g].astype(F32)
                for d in (1, 2, 3):
                    total += recv2[half, n, d - 1, g].astype(F32)
                at_rows = pl.ds(pl.multiple_of(half * 64 + g * 16, 16), 16)
                power[at_rows, :] = total[0] * total[0] + total[1] * total[1] - total[2]
                return carry

            lax.fori_loop(0, 4, finish, 0)
        value = power[...]
        high = value.astype(BF)
        low = (value - high.astype(F32)).astype(BF)
        onehot = bins_ref[...]
        binned = jnp.dot(onehot, high, preferred_element_type=F32)
        binned += jnp.dot(onehot, low, preferred_element_type=F32)
        zsend[:, :, pl.ds(n * 128, 128)] = binned.reshape(16, 8, 128)

    me = z * 2 + c
    spread = []
    for i, (d, e) in enumerate(z_offsets):
        dest = lax.rem(z + d, 8) * 2 + lax.rem(c + e, 2)
        cp = pltpu.make_async_remote_copy(
            src_ref=zsend.at[dest],
            dst_ref=zrecv.at[c, d],
            send_sem=zs_sem.at[i],
            recv_sem=zr_sem.at[i],
            device_id=z_peer(d, e),
            device_id_type=MESH,
        )
        cp.start()
        spread.append(cp)
    zrecv[c, 0] = zsend[me]
    for cp in spread:
        cp.wait_recv()

    parts = []
    for parity in range(2):
        total = zrecv[parity, 0]
        for d in range(1, 8):
            total += zrecv[parity, d]
        parts.append(total)
    even, odd = parts
    row = lax.broadcasted_iota(jnp.int32, (256, 256), 0)
    col = lax.broadcasted_iota(jnp.int32, (256, 256), 1)
    step = col // 2
    from_even = lax.rem(col, 2) == 0
    up = (row == jnp.where(from_even, step, 128 + step)).astype(BF)
    down = (row == jnp.where(from_even, lax.rem(128 - step, 128), 255 - step)).astype(BF)

    def shuffled(value, perm):
        a = value.astype(BF)
        rest = value - a.astype(F32)
        b = rest.astype(BF)
        cc = (rest - b.astype(F32)).astype(BF)
        out = jnp.dot(a, perm, preferred_element_type=F32)
        out += jnp.dot(b, perm, preferred_element_type=F32)
        return out + jnp.dot(cc, perm, preferred_element_type=F32)

    def cut(value, n):
        return value[:, n * 128 : (n + 1) * 128]

    for n in range(NC):
        plus = shuffled(jnp.concatenate([cut(even, n), cut(odd, n)], axis=1), up)
        even_down = jnp.where(lane == 0, cut(even, (3 - n) % 3), cut(even, 2 - n))
        minus = shuffled(jnp.concatenate([even_down, cut(odd, 2 - n)], axis=1), down)
        for g in range(2):
            out_ref[g, :, pl.ds(n * 256, 256)] = plus[2 * g : 2 * g + 2] * inv_ref[g]
            out_ref[g, :, pl.ds(H + n * 256, 256)] = minus[4 + 2 * g : 6 + 2 * g] * inv_ref[g]

    for cp in exchange + spread:
        cp.wait_send()
    for n in range(NC):
        for half in range(2):
            for d in (1, 2, 3):
                first(half, n, d).wait_send()
                second(half, n, d).wait_send()


def on_device(visibility, channel_flags, time_bins, baseline_group_index, owner_map):
    bl = lax.axis_index("bl")
    chip, core = bl // 2, bl % 2
    groups = jnp.arange(64, dtype=jnp.int32)
    own = lax.dynamic_slice_in_dim(baseline_group_index, bl * NB, NB)
    other = lax.dynamic_slice_in_dim(baseline_group_index, (chip * 2 + 1 - core) * NB, NB)
    local = jnp.concatenate([own, other])
    row_of = (owner_map[None, :] == groups[:, None]).astype(F32)
    group_of = (local[None, :] == groups[:, None]).astype(F32)
    member = jnp.dot(row_of, group_of, preferred_element_type=F32)
    before = (groups[:, None] < groups[None, :]).astype(F32)
    rank = jnp.dot(member, before, preferred_element_type=F32)
    slots = jnp.arange(4, dtype=jnp.int32).astype(F32)
    chosen = member[:, None, :] * (rank[:, None, :] == slots[None, :, None]).astype(F32)
    offset = jnp.sum(chosen * (64 - groups).astype(F32)[None, None, :], axis=2)
    idx = (64.0 - offset).astype(jnp.int32)
    totals = jnp.sum(
        (baseline_group_index[None, :] == groups[:, None]).astype(F32), axis=1
    )
    mine = bl * 2 + jnp.arange(2, dtype=jnp.int32)
    count = jnp.sum((owner_map[None, :] == mine[:, None]).astype(F32) * totals[None, :], axis=1)
    inverse = 1.0 / (count * (count - 1.0))

    r = jnp.arange(128, dtype=jnp.int32)
    r_bin = (r // 16) * 2 + r % 2
    r_half, r_group = (r // 4) % 2, ((r // 8) % 2) * 2 + (r // 2) % 2
    k_half, k_group = r // 64, (r // 16) % 4
    k_bin = jnp.tile(time_bins, 8)
    bins = (
        (r_bin[:, None] == k_bin[None, :])
        & (r_half[:, None] == k_half[None, :])
        & (r_group[:, None] == k_group[None, :])
    ).astype(BF)

    tab = jnp.asarray(tables())
    taper = jnp.asarray(taper_row())
    smem = pl.BlockSpec(memory_space=pltpu.SMEM)
    vmem = pl.BlockSpec(memory_space=pltpu.VMEM)
    anym = pl.BlockSpec(memory_space=pl.ANY)
    dma = pltpu.SemaphoreType.DMA
    return pl.pallas_call(
        kernel,
        out_shape=jax.ShapeDtypeStruct((2, 2, F), F32),
        in_specs=[smem, smem, anym, anym, vmem, vmem, vmem],
        out_specs=vmem,
        scratch_shapes=[
            pltpu.VMEM((NB, 32, F), BF),
            pltpu.VMEM((32, F), F32),
            pltpu.VMEM((2, NB * 32, H), BF),
            pltpu.VMEM((NB * 32, H), BF),
            pltpu.VMEM((H, NC * 256), BF),
            pltpu.VMEM((512, 128), F32),
            pltpu.VMEM((512, 128), F32),
            pltpu.VMEM((2 * NB + 1, 6, 16, 128), F32),
            pltpu.VMEM((2, NC, 4, 16, 3, 16, 128), BF),
            pltpu.VMEM((2, NC, 3, 16, 3, 16, 128), BF),
            pltpu.VMEM((2, NC, 4, 4, 3, 16, 128), BF),
            pltpu.VMEM((2, NC, 3, 4, 3, 16, 128), BF),
            pltpu.VMEM((128, 128), F32),
            pltpu.VMEM((16, 8, NC * 128), F32),
            pltpu.VMEM((2, 8, 8, NC * 128), F32),
            dma((PIECES,)),
            dma,
            dma((PIECES,)),
            dma((PIECES,)),
            dma((2, NC, 3)),
            dma((2, NC, 3)),
            dma((2, NC, 3)),
            dma((2, NC, 3)),
            dma((15,)),
            dma((15,)),
        ],
        compiler_params=pltpu.CompilerParams(
            collective_id=0, has_side_effects=True, vmem_limit_bytes=56 << 20
        ),
        name="spectra_power",
    )(idx, inverse, visibility, tab, channel_flags, taper, bins)


def solution(mesh):
    in_specs = (P("bl", "lst", None, None), P("lst", None), P("lst"), P(), P())
    out_specs = P("bl", "lst", None)
    return jax.shard_map(
        on_device, mesh=mesh, in_specs=in_specs, out_specs=out_specs, check_vma=False
    )
```

time: 439 us -> 69.4 us (0.16)
  the two profiles are of different devices: /device:TPU:2 before, /device:TPU:1 now
where the time goes in v1:
time: 69.4 us; the launch traced here: 69.1 us
  Pallas kernels  61.3 us (88%)
  local copies, waits for them, and re-layouts  3.62 us (5%)
  other arithmetic  3.2 us (5%)
  matrix products  0.92 us (1%)
    pallas_call x1, Pallas kernels, on_device(): pl.pallas_call(kernel, out_shape=jax.ShapeDtypeStruct((2, 2, F), F32), in...  61.3 us

profile of v1, /device:TPU:1, one launch (start us, length us, event | category | flops | bytes accessed | tf_op | source)
XLA Modules:
  0.0 69.1 jit_solution(18057761490518679898)
XLA Ops:
  0.0 0.8 %fusion.14 = (s32[32]{0:T(128)S(1)}, s32[32]{0:T(128)S(1)}) fusion(s32[1024]{0:T(1024)} %param.10, s32[]{:T(128)S(6)} %select_n.103, s32[]{:T(128)S(6)} %select_n.106), kind=kLoop, calls=%fused_computation.57 | loop fusion | bytes 520 | tf_op jit(solution)/shard_map/dynamic_slice | solution.py:321
  0.8 0.1 pad_add_fusion
  0.9 0.8 %fusion = f32[64,64]{1,0:T(8,128)S(1)} fusion(s32[64]{0:T(128)S(1)} %pad_add_fusion, s32[64]{0:T(128)} %param.11), kind=kOutput, calls=%fused_computation.7 | convolution fusion | flops 532480 | bytes 16896 | tf_op jit(solution)/shard_map/dot_general | solution.py:326
  1.7 0.1 fusion.1
  1.8 0.2 multiply_reduce_fusion
  2.0 0.7 %copy.10.idx_ref = s32[64,4]{1,0:T(8,128)} copy(s32[64,4]{0,1:T(4,128)S(1)} %subtract_convert_fusion) | data formatting | bytes 2048 | tf_op jit(solution)/shard_map/convert_element_type | solution.py:332
  2.7 0.8 %convert_reduce_fusion = f32[64]{0:T(128)S(1)} fusion(s32[1024]{0:T(1024)} %param.10), kind=kLoop, calls=%fused_computation | loop fusion | flops 196544 | bytes 4352 | tf_op jit(solution)/shard_map/reduce_sum | solution.py:333
  3.6 0.8 %fusion.4 = f32[2]{0:T(128)S(1)} fusion(f32[64]{0:T(128)S(1)} %convert_reduce_fusion, s32[64]{0:T(128)} %param.11, s32[2]{0:T(128)S(1)} %iota_add_fusion), kind=kLoop, calls=%fused_computation.35 | loop fusion | flops 382 | bytes 528 | tf_op jit(solution)/shard_map/reduce_sum | solution.py:337
  4.4 0.5 fusion.7.inv_ref
  4.9 0.7 tile.2
  5.6 0.1 eq.133
  5.7 0.7 %and_convert_fusion.bins_ref = bf16[128,128]{1,0:T(8,128)(2,1)} fusion(s32[128]{0:T(128)S(1)} %get-tuple-element.7, s32[128]{0:T(128)S(1)} %get-tuple-element.8, s32[128]{0:T(128)S(1)} %eq.133, s32[128]{0:T(128)S(1)} %fusion.6, s32[128]{0:T(128)S(1)} %get-tuple-element.9, s32[128]{0:T(128)S(1)} %get-tuple-element.10), kind=kLoop, calls=%fused_computation.3 | loop fusion | flops 98304 | bytes 35840 | tf_op jit(solution)/shard_map/convert_element_type | solution.py:349
  6.4 61.3 %spectra_power.1 = f32[2,2,1536]{2,1,0:T(2,128)} custom-call(s32[64,4]{1,0:T(8,128)} %copy.10.idx_ref, f32[2]{0:T(128)} %fusion.7.inv_ref, bf16[32,16,2,1536]{3,2,1,0:T(2,128)(2,1)} %vis_ref.1, bf16[2,768,768]{2,1,0:T(8,128)(2,1)} %constant.150.clone.tab_hbm, s32[16,1536]{1,0:T(8,128)} %flags_ref.1, f32[1,1536]{1,0:T(1,128)} %constant.151.clone.taper_ref, ...), custom_call_target="tpu_custom_call" | custom-call | tf_op jit(solution)/shard_map/spectra_power/pallas_call | solution.py:357
  67.7 1.3 %copy.12 = f32[2,2,1536]{2,1,0:T(2,128)} copy(f32[2,2,1536]{2,1,0:T(2,128)} %spectra_power.1) | data formatting | bytes 49152
  (7 shorter events, 0.0 us)

commit v2 on v1

--- a/solution.py
+++ b/solution.py
@@ -48,10 +48,13 @@
 
 
 def kernel(
-    idx_ref, inv_ref, vis_ref, tab_hbm, flags_ref, taper_ref, bins_ref,
+    vis_ref, tab_hbm, flags_ref, taper_ref, times_ref, group_ref, owner_ref,
     out_ref,
-    xv, w2, yall, ysend, tab, ra, rb, planes, send1, recv1, send2, recv2, power, zsend, zrecv,
-    ld_sem, tab_sem, ys_sem, yr_sem, s1_sem, r1_sem, s2_sem, r2_sem, zs_sem, zr_sem,
+    idx_v, idx_ref, bins_ref, inv_ref,
+    xv, w2, yall, ysend, tab, ra, rb, planes, send1, recvf, recv1, send2, recv2,
+    power, zsend, zrecv,
+    ld_sem, tab_sem, idx_sem, ys_sem, yr_sem, s1_sem, r1_sem, s2_sem, r2_sem,
+    zs_sem, zr_sem,
 ):
     bl = lax.axis_index("bl")
     z = lax.axis_index("lst")
@@ -124,31 +127,105 @@
         )
         cp.start()
         exchange.append(cp)
+
+    def iota(shape, dim):
+        return lax.broadcasted_iota(jnp.int32, shape, dim)
+
+    def dot(a, b):
+        return jnp.dot(a, b, preferred_element_type=F32)
+
+    def flag(condition):
+        return condition.astype(F32).astype(BF)
+
+    chip = bl // 2
+    groups = group_ref[pl.ds(chip // 2, 1), :]
+    here = iota((64, 128), 1) // 64 == lax.rem(chip, 2)
+    group_of = flag((iota((64, 128), 0) == groups) & here)
+    row_of = flag(iota((64, 64), 0) == owner_ref[...])
+    member = dot(row_of, group_of)
+    rank = dot(member.astype(BF), flag(iota((128, 128), 0) < iota((128, 128), 1)))
+    place = lax.rem(iota((128, 128), 0) + 32 * c, 64)
+    offset = jnp.zeros((64, 128), F32)
+    for s in range(4):
+        weight = jnp.where(iota((128, 128), 1) == s, 64 - place, 0).astype(F32).astype(BF)
+        offset += dot(flag((member > 0.5) & (rank == float(s))), weight)
+    idx_v[...] = 64 - offset.astype(jnp.int32)
+    idx_cp = pltpu.make_async_copy(idx_v, idx_ref, idx_sem)
+    idx_cp.start()
+
+    def late_tables():
+        seen = jnp.zeros((64, 128), F32)
+        for r in range(8):
+            seen += (iota((64, 128), 0) == group_ref[pl.ds(r, 1), :]).astype(F32)
+        totals = dot(seen.astype(BF), jnp.ones((128, 128), BF))
+        mine8 = 2 * bl + lax.rem(iota((8, 64), 0) // 2, 2)
+        count = dot(flag(owner_ref[...] == mine8), totals.astype(BF))
+        inv_ref[...] = 1.0 / (count * (count - 1.0))
+
+        times = times_ref[...].astype(F32).astype(BF)
+        spread_times = flag(lax.rem(iota((16, 128), 1), 16) == iota((16, 128), 0))
+        k_bin = dot(times, spread_times).astype(jnp.int32)
+        r, k = iota((128, 128), 0), iota((128, 128), 1)
+        bins_ref[...] = flag(
+            ((r // 16) * 2 + lax.rem(r, 2) == k_bin)
+            & (lax.rem(r // 4, 2) == k // 64)
+            & (lax.rem(r // 8, 2) * 2 + lax.rem(r // 2, 2) == lax.rem(k // 16, 4))
+        )
+
     tab_cp.wait()
 
-    def first(half, n, d):
-        peer = x_peer(d) if half == 0 else y_peer(d)
-        mine = x if half == 0 else y
+    def peer1(half, d):
+        return x_peer(d) if half == 0 else y_peer(d)
+
+    def peer2(half, d):
+        return y_peer(d) if half == 0 else x_peer(d)
+
+    def mine1(half):
+        return x if half == 0 else y
+
+    def mine2(half):
+        return y if half == 0 else x
+
+    def remote(src, dst, send_sem, recv_sem, device):
         return pltpu.make_async_remote_copy(
-            src_ref=send1.at[half, n, lax.rem(mine + d, 4)],
-            dst_ref=recv1.at[half, n, d - 1],
-            send_sem=s1_sem.at[half, n, d - 1],
-            recv_sem=r1_sem.at[half, n, d - 1],
-            device_id=peer,
+            src_ref=src,
+            dst_ref=dst,
+            send_sem=send_sem,
+            recv_sem=recv_sem,
+            device_id=device,
             device_id_type=MESH,
         )
 
+    def first(half, n, kind, way):
+        d = (1, 3)[way]
+        dest = lax.rem(mine1(half) + (2 if kind == 0 else d), 4)
+        start = 8 * way if kind != 1 else 8 * (1 - way)
+        some = pl.ds(start, 8)
+        src = send1.at[half, n, dest, some]
+        dst = recvf.at[half, n, way] if kind == 0 else recv1.at[half, n, way, some]
+        sems = (s1_sem.at[half, n, kind, way], r1_sem.at[half, n, kind, way])
+        return remote(src, dst, *sems, peer1(half, d))
+
     def second(half, n, d):
-        peer = y_peer(d) if half == 0 else x_peer(d)
-        mine = y if half == 0 else x
-        return pltpu.make_async_remote_copy(
-            src_ref=send2.at[half, n, lax.rem(mine + d, 4)],
-            dst_ref=recv2.at[half, n, d - 1],
-            send_sem=s2_sem.at[half, n, d - 1],
-            recv_sem=r2_sem.at[half, n, d - 1],
-            device_id=peer,
-            device_id_type=MESH,
-        )
+        sems = (s2_sem.at[half, n, d - 1], r2_sem.at[half, n, d - 1])
+        src = send2.at[half, n, lax.rem(mine2(half) + d, 4)]
+        return remote(src, recv2.at[half, n, d - 1], *sems, peer2(half, d))
+
+    def enhance(n):
+        for half in range(2):
+            for way in range(2):
+                first(half, n, 0, way).wait_recv()
+                dest = lax.rem(mine1(half) + (1, 3)[way], 4)
+
+                def add(i, carry):
+                    at_row = way * 8 + i
+                    total = send1[half, n, dest, at_row].astype(F32)
+                    total += recvf[half, n, way, i].astype(F32)
+                    send1[half, n, dest, at_row] = total.astype(BF)
+                    return carry
+
+                lax.fori_loop(0, 8, add, 0, unroll=2)
+                first(half, n, 2, way).start()
 
     lane = lax.broadcasted_iota(jnp.int32, (1, 128), 1)
     for n in range(NC):
@@ -191,12 +268,15 @@
                     planes[at_b, 5] = mr * mr + mi * mi
                     return carry
 
-                return lax.fori_loop(0, 16, split, carry)
+                return lax.fori_loop(0, 16, split, carry, unroll=2)
 
             lax.fori_loop(0, 2, transform, 0)
 
+        if n == 0:
+            idx_cp.wait()
+
         def gather(q, carry):
-            members = [idx_ref[q, s] for s in range(4)]
+            members = [jnp.clip(idx_ref[q, s], 0, 2 * NB) for s in range(4)]
             qx, qy, qg = q // 16, lax.rem(q // 4, 4), lax.rem(q, 4)
             for plane in range(6):
                 total = planes[members[0], plane] + planes[members[1], plane]
@@ -208,25 +288,31 @@
                     send1[1, n, qy, qx * 4 + qg, plane - 3] = total
             return carry
 
-        lax.fori_loop(0, 64, gather, 0)
-        for d in (2, 1, 3):
+        lax.fori_loop(0, 64, gather, 0, unroll=4)
+        for kind in (0, 1):
             for half in range(2):
-                first(half, n, d).start()
+                for way in range(2):
+                    first(half, n, kind, way).start()
+        if n == 0:
+            late_tables()
+        if n > 0:
+            enhance(n - 1)
+    enhance(NC - 1)
 
     for n in range(NC):
         for half in range(2):
-            for d in (1, 2, 3):
-                first(half, n, d).wait_recv()
-            mine = x if half == 0 else y
+            for kind in (1, 2):
+                for way in range(2):
+                    first(half, n, kind, way).wait_recv()
 
             def combine(i, carry):
-                total = send1[half, n, mine, i].astype(F32)
-                for d in (1, 2, 3):
-                    total += recv1[half, n, d - 1, i].astype(F32)
+                total = send1[half, n, mine1(half), i].astype(F32)
+                total += recv1[half, n, 0, i].astype(F32)
+                total += recv1[half, n, 1, i].astype(F32)
                 send2[half, n, i // 4, lax.rem(i, 4)] = total.astype(BF)
                 return carry
 
-            lax.fori_loop(0, 16, combine, 0)
+            lax.fori_loop(0, 16, combine, 0, unroll=2)
             for d in (2, 1, 3):
                 second(half, n, d).start()
 
@@ -234,10 +320,8 @@
         for half in range(2):
             for d in (1, 2, 3):
                 second(half, n, d).wait_recv()
-            mine = y if half == 0 else x
-
             def finish(g, carry):
-                total = send2[half, n, mine, g].astype(F32)
+                total = send2[half, n, mine2(half), g].astype(F32)
                 for d in (1, 2, 3):
                     total += recv2[half, n, d - 1, g].astype(F32)
                 at_rows = pl.ds(pl.multiple_of(half * 64 + g * 16, 16), 16)
@@ -245,12 +329,13 @@
                 return carry
 
             lax.fori_loop(0, 4, finish, 0)
-        value = power[...]
-        high = value.astype(BF)
-        low = (value - high.astype(F32)).astype(BF)
-        onehot = bins_ref[...]
-        binned = jnp.dot(onehot, high, preferred_element_type=F32)
-        binned += jnp.dot(onehot, low, preferred_element_type=F32)
+
+        def binned_by(table, value):
+            high = value.astype(BF)
+            low = (value - high.astype(F32)).astype(BF)
+            return dot(table, high) + dot(table, low)
+
+        binned = binned_by(bins_ref[...], power[...])
         zsend[:, :, pl.ds(n * 128, 128)] = binned.reshape(16, 8, 128)
 
     me = z * 2 + c
@@ -276,7 +361,7 @@
         total = zrecv[parity, 0]
         for d in range(1, 8):
             total += zrecv[parity, d]
-        parts.append(total)
+        parts.append(total * jnp.concatenate([inv_ref[...]] * NC, axis=1))
     even, odd = parts
     row = lax.broadcasted_iota(jnp.int32, (256, 256), 0)
     col = lax.broadcasted_iota(jnp.int32, (256, 256), 1)
@@ -302,64 +387,36 @@
         even_down = jnp.where(lane == 0, cut(even, (3 - n) % 3), cut(even, 2 - n))
         minus = shuffled(jnp.concatenate([even_down, cut(odd, 2 - n)], axis=1), down)
         for g in range(2):
-            out_ref[g, :, pl.ds(n * 256, 256)] = plus[2 * g : 2 * g + 2] * inv_ref[g]
-            out_ref[g, :, pl.ds(H + n * 256, 256)] = minus[4 + 2 * g : 6 + 2 * g] * inv_ref[g]
+            out_ref[g, :, pl.ds(n * 256, 256)] = plus[2 * g : 2 * g + 2]
+            out_ref[g, :, pl.ds(H + n * 256, 256)] = minus[4 + 2 * g : 6 + 2 * g]
 
     for cp in exchange + spread:
         cp.wait_send()
-    for n in range(NC):
-        for half in range(2):
+    for half in range(2):
+        for n in range(NC):
             for d in (1, 2, 3):
-                first(half, n, d).wait_send()
                 second(half, n, d).wait_send()
+            for kind in range(3):
+                for way in range(2):
+                    first(half, n, kind, way).wait_send()
 
 
 def on_device(visibility, channel_flags, time_bins, baseline_group_index, owner_map):
-    bl = lax.axis_index("bl")
-    chip, core = bl // 2, bl % 2
-    groups = jnp.arange(64, dtype=jnp.int32)
-    own = lax.dynamic_slice_in_dim(baseline_group_index, bl * NB, NB)
-    other = lax.dynamic_slice_in_dim(baseline_group_index, (chip * 2 + 1 - core) * NB, NB)
-    local = jnp.concatenate([own, other])
-    row_of = (owner_map[None, :] == groups[:, None]).astype(F32)
-    group_of = (local[None, :] == groups[:, None]).astype(F32)
-    member = jnp.dot(row_of, group_of, preferred_element_type=F32)
-    before = (groups[:, None] < groups[None, :]).astype(F32)
-    rank = jnp.dot(member, before, preferred_element_type=F32)
-    slots = jnp.arange(4, dtype=jnp.int32).astype(F32)
-    chosen = member[:, None, :] * (rank[:, None, :] == slots[None, :, None]).astype(F32)
-    offset = jnp.sum(chosen * (64 - groups).astype(F32)[None, None, :], axis=2)
-    idx = (64.0 - offset).astype(jnp.int32)
-    totals = jnp.sum(
-        (baseline_group_index[None, :] == groups[:, None]).astype(F32), axis=1
-    )
-    mine = bl * 2 + jnp.arange(2, dtype=jnp.int32)
-    count = jnp.sum((owner_map[None, :] == mine[:, None]).astype(F32) * totals[None, :], axis=1)
-    inverse = 1.0 / (count * (count - 1.0))
-
-    r = jnp.arange(128, dtype=jnp.int32)
-    r_bin = (r // 16) * 2 + r % 2
-    r_half, r_group = (r // 4) % 2, ((r // 8) % 2) * 2 + (r // 2) % 2
-    k_half, k_group = r // 64, (r // 16) % 4
-    k_bin = jnp.tile(time_bins, 8)
-    bins = (
-        (r_bin[:, None] == k_bin[None, :])
-        & (r_half[:, None] == k_half[None, :])
-        & (r_group[:, None] == k_group[None, :])
-    ).astype(BF)
-
     tab = jnp.asarray(tables())
     taper = jnp.asarray(taper_row())
-    smem = pl.BlockSpec(memory_space=pltpu.SMEM)
     vmem = pl.BlockSpec(memory_space=pltpu.VMEM)
     anym = pl.BlockSpec(memory_space=pl.ANY)
     dma = pltpu.SemaphoreType.DMA
     return pl.pallas_call(
         kernel,
         out_shape=jax.ShapeDtypeStruct((2, 2, F), F32),
-        in_specs=[smem, smem, anym, anym, vmem, vmem, vmem],
+        in_specs=[anym, anym, vmem, vmem, vmem, vmem, vmem],
         out_specs=vmem,
         scratch_shapes=[
+            pltpu.VMEM((64, 128), jnp.int32),
+            pltpu.SMEM((64, 128), jnp.int32),
+            pltpu.VMEM((128, 128), BF),
+            pltpu.VMEM((8, 128), F32),
             pltpu.VMEM((NB, 32, F), BF),
             pltpu.VMEM((32, F), F32),
             pltpu.VMEM((2, NB * 32, H), BF),
@@ -369,7 +426,8 @@
             pltpu.VMEM((512, 128), F32),
             pltpu.VMEM((2 * NB + 1, 6, 16, 128), F32),
             pltpu.VMEM((2, NC, 4, 16, 3, 16, 128), BF),
-            pltpu.VMEM((2, NC, 3, 16, 3, 16, 128), BF),
+            pltpu.VMEM((2, NC, 2, 8, 3, 16, 128), BF),
+            pltpu.VMEM((2, NC, 2, 16, 3, 16, 128), BF),
             pltpu.VMEM((2, NC, 4, 4, 3, 16, 128), BF),
             pltpu.VMEM((2, NC, 3, 4, 3, 16, 128), BF),
             pltpu.VMEM((128, 128), F32),
@@ -377,10 +435,11 @@
             pltpu.VMEM((2, 8, 8, NC * 128), F32),
             dma((PIECES,)),
             dma,
+            dma,
             dma((PIECES,)),
             dma((PIECES,)),
-            dma((2, NC, 3)),
-            dma((2, NC, 3)),
+            dma((2, NC, 3, 2)),
+            dma((2, NC, 3, 2)),
             dma((2, NC, 3)),
             dma((2, NC, 3)),
             dma((15,)),
@@ -390,7 +449,15 @@
             collective_id=0, has_side_effects=True, vmem_limit_bytes=56 << 20
         ),
         name="spectra_power",
-    )(idx, inverse, visibility, tab, channel_flags, taper, bins)
+    )(
+        visibility,
+        tab,
+        channel_flags,
+        taper,
+        time_bins.reshape(1, 16),
+        baseline_group_index.reshape(8, 128),
+        owner_map.reshape(1, 64),
+    )
 
 
 def solution(mesh):

time: 69.4 us -> 56.1 us (0.81)
  Pallas kernels: 61.3 us -> 54.6 us
  other arithmetic: 3.2 us -> 0 us
  local copies, waits for them, and re-layouts: 3.62 us -> 1.35 us
  matrix products: 0.92 us -> 0 us
    pallas_call x1, Pallas kernels: 61.3 us -> 54.6 us  [on_device(): pl.pallas_call(kernel, out_shape=jax.ShapeDtypeStruct((2, 2, F), F32), in...]
    reduce_sum x3 -> x0, other arithmetic: 1.84 us -> none  [the longest x1 0.85 us: on_device(): jnp.sum((owner_map[None, :] == mine[:, None]).astype(F32) * totals[None,...]
    dot_general x2 -> x0, matrix products: 0.92 us -> none  [the longest x1 0.79 us: on_device(): member = jnp.dot(row_of, group_of, preferred_element_type=F32)]
    dynamic_slice x1 -> x0, local copies, waits for them, and re-layouts: 0.83 us -> none  [on_device(): own = lax.dynamic_slice_in_dim(baseline_group_index, bl * NB, NB)]
    convert_element_type x4 -> x0, other arithmetic: 0.74 us -> none  [the longest x1 0.73 us: on_device(): bins = ((r_bin[:, None] == k_bin[None, :]) & (r_half[:, None] == k_half[N...]
    convert_element_type x1 -> x0, local copies, waits for them, and re-layouts: 0.7 us -> none  [on_device(): idx = (64.0 - offset).astype(jnp.int32)]
where the time goes in v2:
time: 56.1 us; the launch traced here: 56 us
  Pallas kernels  54.6 us (97%)
  local copies, waits for them, and re-layouts  1.35 us (2%)
    pallas_call x1, Pallas kernels, on_device(): pl.pallas_call(kernel, out_shape=jax.ShapeDtypeStruct((2, 2, F), F32), in...  54.6 us
    unnamed x1, local copies, waits for them, and re-layouts  1.35 us

profile of v2, /device:TPU:1, one launch (start us, length us, event | category | flops | bytes accessed | tf_op | source)
XLA Modules:
  0.0 56.0 jit_solution(4292785116367482487)
XLA Ops:
  0.0 54.6 %spectra_power.1 = f32[2,2,1536]{2,1,0:T(2,128)} custom-call(bf16[32,16,2,1536]{3,2,1,0:T(2,128)(2,1)} %vis_ref.1, bf16[2,768,768]{2,1,0:T(8,128)(2,1)} %constant.4.clone.tab_hbm, s32[16,1536]{1,0:T(8,128)} %flags_ref.1, f32[1,1536]{1,0:T(1,128)} %constant.5.clone.taper_ref, s32[1,16]{1,0:T(1,128)} %bitcast.4, s32[8,128]{1,0:T(8,128)} %bitcast.3, ...), custom_call_target="tpu_custom_call" | custom-call | tf_op jit(solution)/shard_map/spectra_power/pallas_call | solution.py:410
  54.6 1.3 %copy.9 = f32[2,2,1536]{2,1,0:T(2,128)} copy(f32[2,2,1536]{2,1,0:T(2,128)} %spectra_power.1) | data formatting | bytes 49152

commit v3 on v2

--- a/solution.py
+++ b/solution.py
@@ -210,6 +210,12 @@
         sems = (s2_sem.at[half, n, d - 1], r2_sem.at[half, n, d - 1])
         src = send2.at[half, n, lax.rem(mine2(half) + d, 4)]
         return remote(src, recv2.at[half, n, d - 1], *sems, peer2(half, d))
+
+    def spread(n, i):
+        d, e = z_offsets[i]
+        src = zsend.at[n, lax.rem(z + d, 8) * 2 + lax.rem(c + e, 2)]
+        sems = (zs_sem.at[n, i], zr_sem.at[n, i])
+        return remote(src, zrecv.at[n, c, d], *sems, z_peer(d, e))
 
     def enhance(n):
         for half in range(2):
@@ -275,24 +281,34 @@
         if n == 0:
             idx_cp.wait()
 
-        def gather(q, carry):
+        def gather(q, half, to, at_row):
             members = [jnp.clip(idx_ref[q, s], 0, 2 * NB) for s in range(4)]
-            qx, qy, qg = q // 16, lax.rem(q // 4, 4), lax.rem(q, 4)
-            for plane in range(6):
-                total = planes[members[0], plane] + planes[members[1], plane]
-                total += planes[members[2], plane] + planes[members[3], plane]
-                total = total.astype(BF)
-                if plane < 3:
-                    send1[0, n, qx, qy * 4 + qg, plane] = total
-                else:
-                    send1[1, n, qy, qx * 4 + qg, plane - 3] = total
-            return carry
-
-        lax.fori_loop(0, 64, gather, 0, unroll=4)
-        for kind in (0, 1):
-            for half in range(2):
-                for way in range(2):
-                    first(half, n, kind, way).start()
+            for plane in range(3):
+                p = half * 3 + plane
+                total = planes[members[0], p] + planes[members[1], p]
+                total += planes[members[2], p] + planes[members[3], p]
+                send1[half, n, to, at_row, plane] = total.astype(BF)
+
+        def gather_block(half, d):
+            to = lax.rem(mine1(half) + d, 4)
+
+            def gather_one(i, carry):
+                qx, qy = (to, i // 4) if half == 0 else (i // 4, to)
+                gather(qx * 16 + qy * 4 + lax.rem(i, 4), half, to, i)
+                return carry
+
+            lax.fori_loop(0, 16, gather_one, 0, unroll=4)
+
+        for half in range(2):
+            gather_block(half, 2)
+            for way in range(2):
+                first(half, n, 0, way).start()
+        for half in range(2):
+            for way in range(2):
+                gather_block(half, (1, 3)[way])
+                first(half, n, 1, way).start()
+        for half in range(2):
+            gather_block(half, 0)
         if n == 0:
             late_tables()
         if n > 0:
@@ -336,32 +352,21 @@
             return dot(table, high) + dot(table, low)
 
         binned = binned_by(bins_ref[...], power[...])
-        zsend[:, :, pl.ds(n * 128, 128)] = binned.reshape(16, 8, 128)
-
-    me = z * 2 + c
-    spread = []
-    for i, (d, e) in enumerate(z_offsets):
-        dest = lax.rem(z + d, 8) * 2 + lax.rem(c + e, 2)
-        cp = pltpu.make_async_remote_copy(
-            src_ref=zsend.at[dest],
-            dst_ref=zrecv.at[c, d],
-            send_sem=zs_sem.at[i],
-            recv_sem=zr_sem.at[i],
-            device_id=z_peer(d, e),
-            device_id_type=MESH,
-        )
-        cp.start()
-        spread.append(cp)
-    zrecv[c, 0] = zsend[me]
-    for cp in spread:
-        cp.wait_recv()
-
-    parts = []
-    for parity in range(2):
-        total = zrecv[parity, 0]
-        for d in range(1, 8):
-            total += zrecv[parity, d]
-        parts.append(total * jnp.concatenate([inv_ref[...]] * NC, axis=1))
+        zsend[n] = binned.reshape(16, 8, 128)
+        zrecv[n, c, 0] = zsend[n, z * 2 + c]
+        for i in range(15):
+            spread(n, i).start()
+
+    parts = [[], []]
+    scale = inv_ref[...]
+    for n in range(NC):
+        for i in range(15):
+            spread(n, i).wait_recv()
+        for half in range(2):
+            total = zrecv[n, half, 0]
+            for d in range(1, 8):
+                total += zrecv[n, half, d]
+            parts[half].append(total * scale)
     even, odd = parts
     row = lax.broadcasted_iota(jnp.int32, (256, 256), 0)
     col = lax.broadcasted_iota(jnp.int32, (256, 256), 1)
@@ -379,19 +384,19 @@
         out += jnp.dot(b, perm, preferred_element_type=F32)
         return out + jnp.dot(cc, perm, preferred_element_type=F32)
 
-    def cut(value, n):
-        return value[:, n * 128 : (n + 1) * 128]
-
-    for n in range(NC):
-        plus = shuffled(jnp.concatenate([cut(even, n), cut(odd, n)], axis=1), up)
-        even_down = jnp.where(lane == 0, cut(even, (3 - n) % 3), cut(even, 2 - n))
-        minus = shuffled(jnp.concatenate([even_down, cut(odd, 2 - n)], axis=1), down)
+    for n in range(NC):
+        plus = shuffled(jnp.concatenate([even[n], odd[n]], axis=1), up)
+        even_down = jnp.where(lane == 0, even[(3 - n) % 3], even[2 - n])
+        minus = shuffled(jnp.concatenate([even_down, odd[2 - n]], axis=1), down)
         for g in range(2):
             out_ref[g, :, pl.ds(n * 256, 256)] = plus[2 * g : 2 * g + 2]
             out_ref[g, :, pl.ds(H + n * 256, 256)] = minus[4 + 2 * g : 6 + 2 * g]
 
-    for cp in exchange + spread:
+    for cp in exchange:
         cp.wait_send()
+    for n in range(NC):
+        for i in range(15):
+            spread(n, i).wait_send()
     for half in range(2):
         for n in range(NC):
             for d in (1, 2, 3):
@@ -431,8 +436,8 @@
             pltpu.VMEM((2, NC, 4, 4, 3, 16, 128), BF),
             pltpu.VMEM((2, NC, 3, 4, 3, 16, 128), BF),
             pltpu.VMEM((128, 128), F32),
-            pltpu.VMEM((16, 8, NC * 128), F32),
-            pltpu.VMEM((2, 8, 8, NC * 128), F32),
+            pltpu.VMEM((NC, 16, 8, 128), F32),
+            pltpu.VMEM((NC, 2, 8, 8, 128), F32),
             dma((PIECES,)),
             dma,
             dma,
@@ -442,8 +447,8 @@
             dma((2, NC, 3, 2)),
             dma((2, NC, 3)),
             dma((2, NC, 3)),
-            dma((15,)),
-            dma((15,)),
+            dma((NC, 15)),
+            dma((NC, 15)),
         ],
         compiler_params=pltpu.CompilerParams(
             collective_id=0, has_side_effects=True, vmem_limit_bytes=56 << 20

time: 56.1 us -> 53.4 us (0.952)
  Pallas kernels: 54.6 us -> 51.8 us
    pallas_call x1, Pallas kernels: 54.6 us -> 51.8 us  [on_device(): pl.pallas_call(kernel, out_shape=jax.ShapeDtypeStruct((2, 2, F), F32), in...]
where the time goes in v3:
time: 53.4 us; the launch traced here: 53.2 us
  Pallas kernels  51.8 us (97%)
  local copies, waits for them, and re-layouts  1.35 us (3%)
    pallas_call x1, Pallas kernels, on_device(): pl.pallas_call(kernel, out_shape=jax.ShapeDtypeStruct((2, 2, F), F32), in...  51.8 us
    unnamed x1, local copies, waits for them, and re-layouts  1.35 us

profile of v3, /device:TPU:1, one launch (start us, length us, event | category | flops | bytes accessed | tf_op | source)
XLA Modules:
  0.0 53.2 jit_solution(9465250058672354342)
XLA Ops:
  0.0 51.8 %spectra_power.1 = f32[2,2,1536]{2,1,0:T(2,128)} custom-call(bf16[32,16,2,1536]{3,2,1,0:T(2,128)(2,1)} %vis_ref.1, bf16[2,768,768]{2,1,0:T(8,128)(2,1)} %constant.4.clone.tab_hbm, s32[16,1536]{1,0:T(8,128)} %flags_ref.1, f32[1,1536]{1,0:T(1,128)} %constant.5.clone.taper_ref, s32[1,16]{1,0:T(1,128)} %bitcast.4, s32[8,128]{1,0:T(8,128)} %bitcast.3, ...), custom_call_target="tpu_custom_call" | custom-call | tf_op jit(solution)/shard_map/spectra_power/pallas_call | solution.py:415
  51.9 1.3 %copy.9 = f32[2,2,1536]{2,1,0:T(2,128)} copy(f32[2,2,1536]{2,1,0:T(2,128)} %spectra_power.1) | data formatting | bytes 49152

commit v4 on v3

--- a/solution.py
+++ b/solution.py
@@ -48,12 +48,13 @@
 
 
 def kernel(
-    vis_ref, tab_hbm, flags_ref, taper_ref, times_ref, group_ref, owner_ref,
+    vis_ref, tab_hbm, flags_hbm, taper_hbm, times_hbm, group_hbm, owner_hbm,
     out_ref,
+    flags_ref, taper_ref, times_ref, group_ref, owner_ref, up_ref, down_ref,
     idx_v, idx_ref, bins_ref, inv_ref,
     xv, w2, yall, ysend, tab, ra, rb, planes, send1, recvf, recv1, send2, recv2,
     power, zsend, zrecv,
-    ld_sem, tab_sem, idx_sem, ys_sem, yr_sem, s1_sem, r1_sem, s2_sem, r2_sem,
+    small_sem, ld_sem, tab_sem, idx_sem, ys_sem, yr_sem, s1_sem, r1_sem, s2_sem, r2_sem,
     zs_sem, zr_sem,
 ):
     bl = lax.axis_index("bl")
@@ -76,6 +77,18 @@
 
     z_offsets = [(d, e) for d in range(8) for e in range(2) if d or e]
 
+    pairs = [
+        (flags_hbm, flags_ref),
+        (taper_hbm, taper_ref),
+        (group_hbm, group_ref),
+        (owner_hbm, owner_ref),
+        (times_hbm, times_ref),
+    ]
+    small = []
+    for i, (src, dst) in enumerate(pairs):
+        cp = pltpu.make_async_copy(src, dst, small_sem.at[i])
+        cp.start()
+        small.append(cp)
     rows = vis_ref.reshape(NB, 32, F)
     loads = []
     for p in range(PIECES):
@@ -93,41 +106,12 @@
     for peer in peers:
         pl.semaphore_signal(barrier, inc=1, device_id=peer, device_id_type=MESH)
 
+    small[0].wait()
+    small[1].wait()
     for t in range(16):
         row = taper_ref[...] * flags_ref[pl.ds(t, 1), :].astype(F32)
         w2[pl.ds(2 * t, 2), :] = jnp.broadcast_to(row, (2, F))
     planes[2 * NB] = jnp.zeros((6, 16, 128), F32)
-    sign = (1 - 2 * c).astype(F32)
-
-    pl.semaphore_wait(barrier, len(peers))
-    exchange = []
-    for p in range(PIECES):
-        loads[p].wait()
-
-        def fold(b, carry):
-            for j in range(6):
-                lo_at, hi_at = pl.ds(j * 128, 128), pl.ds(H + j * 128, 128)
-                lo = (xv[b, :, lo_at].astype(F32) * w2[:, lo_at]).astype(BF).astype(F32)
-                hi = (xv[b, :, hi_at].astype(F32) * w2[:, hi_at]).astype(BF).astype(F32)
-                hi = hi * sign
-                at_rows = pl.ds(pl.multiple_of(b * 32, 32), 32)
-                yall[0, at_rows, lo_at] = (lo + hi).astype(BF)
-                ysend[at_rows, lo_at] = (lo - hi).astype(BF)
-            return carry
-
-        lax.fori_loop(p * PB, (p + 1) * PB, fold, 0)
-        piece = pl.ds(p * PB * 32, PB * 32)
-        cp = pltpu.make_async_remote_copy(
-            src_ref=ysend.at[piece],
-            dst_ref=yall.at[1, piece],
-            send_sem=ys_sem.at[p],
-            recv_sem=yr_sem.at[p],
-            device_id=z_peer(0, 1),
-            device_id_type=MESH,
-        )
-        cp.start()
-        exchange.append(cp)
-
     def iota(shape, dim):
         return lax.broadcasted_iota(jnp.int32, shape, dim)
 
@@ -137,6 +121,8 @@
     def flag(condition):
         return condition.astype(F32).astype(BF)
 
+    for cp in small[2:]:
+        cp.wait()
     chip = bl // 2
     groups = group_ref[pl.ds(chip // 2, 1), :]
     here = iota((64, 128), 1) // 64 == lax.rem(chip, 2)
@@ -153,6 +139,37 @@
     idx_cp = pltpu.make_async_copy(idx_v, idx_ref, idx_sem)
     idx_cp.start()
 
+    sign = (1 - 2 * c).astype(F32)
+
+    pl.semaphore_wait(barrier, len(peers))
+    exchange = []
+    for p in range(PIECES):
+        loads[p].wait()
+
+        def fold(b, carry):
+            for j in range(6):
+                lo_at, hi_at = pl.ds(j * 128, 128), pl.ds(H + j * 128, 128)
+                lo = (xv[b, :, lo_at].astype(F32) * w2[:, lo_at]).astype(BF).astype(F32)
+                hi = (xv[b, :, hi_at].astype(F32) * w2[:, hi_at]).astype(BF).astype(F32)
+                hi = hi * sign
+                at_rows = pl.ds(pl.multiple_of(b * 32, 32), 32)
+                yall[0, at_rows, lo_at] = (lo + hi).astype(BF)
+                ysend[at_rows, lo_at] = (lo - hi).astype(BF)
+            return carry
+
+        lax.fori_loop(p * PB, (p + 1) * PB, fold, 0)
+        piece = pl.ds(p * PB * 32, PB * 32)
+        cp = pltpu.make_async_remote_copy(
+            src_ref=ysend.at[piece],
+            dst_ref=yall.at[1, piece],
+            send_sem=ys_sem.at[p],
+            recv_sem=yr_sem.at[p],
+            device_id=z_peer(0, 1),
+            device_id_type=MESH,
+        )
+        cp.start()
+        exchange.append(cp)
+
     def late_tables():
         seen = jnp.zeros((64, 128), F32)
         for r in range(8):
@@ -172,6 +189,14 @@
             & (lax.rem(r // 8, 2) * 2 + lax.rem(r // 2, 2) == lax.rem(k // 16, 4))
         )
 
+        row, col = iota((256, 256), 0), iota((256, 256), 1)
+        step = col // 2
+        from_even = lax.rem(col, 2) == 0
+        up_ref[...] = flag(row == jnp.where(from_even, step, 128 + step))
+        down_ref[...] = flag(
+            row == jnp.where(from_even, lax.rem(128 - step, 128), 255 - step)
+        )
+
     tab_cp.wait()
 
     def peer1(half, d):
@@ -230,7 +255,7 @@
                     send1[half, n, dest, at_row] = total.astype(BF)
                     return carry
 
-                lax.fori_loop(0, 8, add, 0, unroll=2)
+                lax.fori_loop(0, 8, add, 0, unroll=8)
                 first(half, n, 2, way).start()
 
     lane = lax.broadcasted_iota(jnp.int32, (1, 128), 1)
@@ -297,7 +322,7 @@
                 gather(qx * 16 + qy * 4 + lax.rem(i, 4), half, to, i)
                 return carry
 
-            lax.fori_loop(0, 16, gather_one, 0, unroll=4)
+            lax.fori_loop(0, 16, gather_one, 0, unroll=16)
 
         for half in range(2):
             gather_block(half, 2)
@@ -328,7 +353,7 @@
                 send2[half, n, i // 4, lax.rem(i, 4)] = total.astype(BF)
                 return carry
 
-            lax.fori_loop(0, 16, combine, 0, unroll=2)
+            lax.fori_loop(0, 16, combine, 0, unroll=4)
             for d in (2, 1, 3):
                 second(half, n, d).start()
 
@@ -368,12 +393,7 @@
                 total += zrecv[n, half, d]
             parts[half].append(total * scale)
     even, odd = parts
-    row = lax.broadcasted_iota(jnp.int32, (256, 256), 0)
-    col = lax.broadcasted_iota(jnp.int32, (256, 256), 1)
-    step = col // 2
-    from_even = lax.rem(col, 2) == 0
-    up = (row == jnp.where(from_even, step, 128 + step)).astype(BF)
-    down = (row == jnp.where(from_even, lax.rem(128 - step, 128), 255 - step)).astype(BF)
+    up, down = up_ref[...], down_ref[...]
 
     def shuffled(value, perm):
         a = value.astype(BF)
@@ -415,9 +435,16 @@
     return pl.pallas_call(
         kernel,
         out_shape=jax.ShapeDtypeStruct((2, 2, F), F32),
-        in_specs=[anym, anym, vmem, vmem, vmem, vmem, vmem],
+        in_specs=[anym] * 7,
         out_specs=vmem,
         scratch_shapes=[
+            pltpu.VMEM((16, F), jnp.int32),
+            pltpu.VMEM((1, F), F32),
+            pltpu.VMEM((1, 16), jnp.int32),
+            pltpu.VMEM((8, 128), jnp.int32),
+            pltpu.VMEM((1, 64), jnp.int32),
+            pltpu.VMEM((256, 256), BF),
+            pltpu.VMEM((256, 256), BF),
             pltpu.VMEM((64, 128), jnp.int32),
             pltpu.SMEM((64, 128), jnp.int32),
             pltpu.VMEM((128, 128), BF),
@@ -438,6 +465,7 @@
             pltpu.VMEM((128, 128), F32),
             pltpu.VMEM((NC, 16, 8, 128), F32),
             pltpu.VMEM((NC, 2, 8, 8, 128), F32),
+            dma((5,)),
             dma((PIECES,)),
             dma,
             dma,

time: 53.4 us -> 52.2 us (0.978)
  Pallas kernels: 51.8 us -> 50.7 us
    pallas_call x1, Pallas kernels: 51.8 us -> 50.7 us  [on_device(): pl.pallas_call(kernel, out_shape=jax.ShapeDtypeStruct((2, 2, F), F32), in...]
where the time goes in v4:
time: 52.2 us; the launch traced here: 52.1 us
  Pallas kernels  50.7 us (97%)
  local copies, waits for them, and re-layouts  1.35 us (3%)
    pallas_call x1, Pallas kernels, on_device(): pl.pallas_call(kernel, out_shape=jax.ShapeDtypeStruct((2, 2, F), F32), in...  50.7 us
    unnamed x1, local copies, waits for them, and re-layouts  1.35 us

profile of v4, /device:TPU:1, one launch (start us, length us, event | category | flops | bytes accessed | tf_op | source)
XLA Modules:
  0.0 52.1 jit_solution(12704612582380764098)
XLA Ops:
  0.0 50.7 %spectra_power.1 = f32[2,2,1536]{2,1,0:T(2,128)} custom-call(bf16[32,16,2,1536]{3,2,1,0:T(2,128)(2,1)} %vis_ref.1, bf16[2,768,768]{2,1,0:T(8,128)(2,1)} %constant.4.clone.tab_hbm, s32[16,1536]{1,0:T(8,128)} %flags_hbm.1, f32[1,1536]{1,0:T(1,128)} %constant.5.clone.taper_hbm, s32[1,16]{1,0:T(1,128)} %bitcast.4, s32[8,128]{1,0:T(8,128)} %bitcast.3, ...), custom_call_target="tpu_custom_call" | custom-call | tf_op jit(solution)/shard_map/spectra_power/pallas_call | solution.py:435
  50.7 1.3 %copy.9 = f32[2,2,1536]{2,1,0:T(2,128)} copy(f32[2,2,1536]{2,1,0:T(2,128)} %spectra_power.1) | data formatting | bytes 49152
